TPU v7x, 128 devices: a whole 4x4x4 slice. The times are simulated.
128 devices in a mesh: row: 4 (over z), col: 32 (over x, y, core).
Axes of the slice: x: 4, y: 4, z: 4, core: 2. Of those that a mesh axis runs over, the one named last changes fastest.
Arguments:
- scan: float32 [4096, 32768], P('row', 'col'), may hold values from -6 to 6
- anchors: int32 [2, 8, 32, 2], P(None, 'row', 'col'), may hold values from -1 to 32256, as said below
- targets: int32 [2, 8, 32], P(None, 'row', 'col'), may hold values from 0 to 8
- stem_weight: bfloat16 [7, 7, 1, 64], replicated, may hold values from -0.875 to 0.875
- stem_bias: float32 [64], replicated, may hold values from -3 to 3
- conv1_weight: bfloat16 [3, 3, 64, 64], replicated, may hold values from -0.25 to 0.25
- conv1_bias: float32 [64], replicated, may hold values from -3 to 3
- conv2_weight: bfloat16 [3, 3, 64, 64], replicated, may hold values from -0.25 to 0.25
- conv2_bias: float32 [64], replicated, may hold values from -3 to 3
- head_weight: bfloat16 [64, 9], replicated, may hold values from -0.75 to 0.75
- head_bias: float32 [9], replicated, may hold values from -4 to 4
Outputs:
- saliency: float32 [4096, 32768], P('row', 'col')
- class_scores: float32 [2, 8, 32], P(None, 'row', 'col')
Inputs may be any that keep to these rules, and one draw needn't show every extreme that they name: anchors[p, k, c] is the top-left corner (row, column) of a window lying wholly inside the scan, or has row -1 when the slot is empty. Slots r * 2 to (r + 1) * 2 - 1 of tile column c hold only windows whose corner lies in tile (r, c), that is rows r * 1024 to (r + 1) * 1024 - 1 and columns c * 1024 to (c + 1) * 1024 - 1. In every pass some tile holds 2 live windows and some tile column holds 4; no tile column holds more than 4 live windows in a pass. Every tile column has empty slots in every pass, and empty slots have column c * 1024 + 512.
All inputs are finite; a program needn't handle non-finite values.
Results may differ from a plain program's by a relative error of at most 0.0054.
Values may be sent and summed in bfloat16 or wider, within the bound.
A program may use at most 192 MiB of HBM per device.

v0:
```python
import jax
import jax.numpy as jnp
from jax import lax
from jax.experimental import pallas as pl
from jax.experimental.pallas import tpu as pltpu
from jax.sharding import PartitionSpec as P

TILE = 1024
WIN = 512
RIM = 512
C = 64
F = 128
SLOTS = 4
LOW = -3.0e38
MESH = pl.DeviceIdType.MESH
WAYS = ((0, 0), (0, 1), (1, 0), (1, 1))


def lanes(shape):
    return lax.broadcasted_iota(jnp.int32, shape, len(shape) - 1)


def frame_kernel(
    scan, own, framed, infos,
    raw, pixels, blank_rows, blank_cols, blanks, loads, keeps, up_send, up_recv, left_send, left_recv,
    corner_send, corner_recv, info_send, info_recv,
):
    row, col = lax.axis_index("row"), lax.axis_index("col")
    rows, cols = lax.axis_size("row"), lax.axis_size("col")
    up, down, left, right = row > 0, row < rows - 1, col > 0, col < cols - 1
    chunks = TILE // F
    fetch = [
        pltpu.make_async_copy(scan.at[pl.ds(k * F, F)], raw.at[pl.ds(k * F, F)], loads.at[k])
        for k in range(chunks)
    ]
    for copy in fetch:
        copy.start()
    infos[...] = jnp.full_like(infos, -1)
    infos[0] = own[...]

    blank_rows[...] = jnp.zeros_like(blank_rows)
    blank_cols[...] = jnp.zeros_like(blank_cols)

    def blank(source, k, by_rows, by_cols, there):
        return pltpu.make_async_copy(source, framed.at[by_rows, by_cols], blanks.at[k]), there

    edge, beyond = pl.ds(TILE, 16), pl.ds(TILE, F)
    no_down, no_right = row == rows - 1, col == cols - 1
    clears = (
        blank(blank_rows, 0, edge, pl.ds(0, TILE), no_down),
        blank(blank_rows.at[:, pl.ds(0, RIM)], 1, edge, pl.ds(TILE, RIM), no_down & right),
        blank(blank_cols, 2, pl.ds(0, TILE), beyond, no_right),
        blank(blank_cols.at[pl.ds(0, RIM)], 3, pl.ds(TILE, RIM), beyond, no_right),
    )
    for clear, there in clears:
        pl.when(there)(clear.start)

    barrier = pltpu.get_barrier_semaphore()
    partners = (
        (-1, 0, up), (1, 0, down), (0, -1, left), (0, 1, right),
        (1, 1, down & right), (-1, -1, up & left),
    )
    for by_row, by_col, there in partners:
        @pl.when(there)
        def _():
            pl.semaphore_signal(
                barrier, inc=1, device_id=(row + by_row, col + by_col), device_id_type=MESH
            )
    pl.semaphore_wait(barrier, sum(there.astype(jnp.int32) for _, _, there in partners))

    def remote(source, target, send, recv, by_row, by_col):
        return pltpu.make_async_remote_copy(
            src_ref=source, dst_ref=target, send_sem=send, recv_sem=recv,
            device_id=(row + by_row, col + by_col), device_id_type=MESH,
        )

    def part(k):
        return pl.ds(k * F, F)

    def under(k):
        return pl.ds(TILE + k * F, F)

    ups = [
        remote(pixels.at[part(k % 4), pl.ds(k // 4 * RIM, RIM)],
               framed.at[under(k % 4), pl.ds(k // 4 * RIM, RIM)],
               up_send.at[k], up_recv.at[k], -1, 0)
        for k in range(8)
    ]
    lefts = [
        remote(pixels.at[part(k), pl.ds(0, RIM)], framed.at[part(k), pl.ds(TILE, RIM)],
               left_send.at[k], left_recv.at[k], 0, -1)
        for k in range(chunks)
    ]
    corners = [
        remote(framed.at[under(k), pl.ds(0, RIM)], framed.at[under(k), pl.ds(TILE, RIM)],
               corner_send.at[k], corner_recv.at[k], 0, -1)
        for k in range(RIM // F)
    ]
    tells = [
        (remote(own, infos.at[1], info_send.at[0], info_recv.at[0], 0, 1), right, left),
        (remote(own, infos.at[2], info_send.at[1], info_recv.at[1], 1, 0), down, up),
        (remote(own, infos.at[3], info_send.at[2], info_recv.at[2], 1, 1), down & right, up & left),
    ]
    kept = [
        pltpu.make_async_copy(pixels.at[part(k)], framed.at[part(k), pl.ds(0, TILE)], keeps.at[k])
        for k in range(chunks)
    ]
    for k in range(chunks):
        fetch[k].wait()
        pixels[k * F : (k + 1) * F, :] = raw[k * F : (k + 1) * F, :].astype(jnp.bfloat16)
        if k < 4:
            pl.when(up)(ups[k].start)
        if k == 3:
            for late in ups[4:]:
                pl.when(up)(late.start)
        pl.when(left)(lefts[k].start)
        kept[k].start()
    for tell, goes, _ in tells:
        pl.when(goes)(tell.start)
    for k in range(len(ups)):
        pl.when(down)(ups[k].wait_recv)
        if k < len(corners):
            pl.when(down & left)(corners[k].start)
    for tell, goes, comes in tells:
        pl.when(goes)(tell.wait_send)
        pl.when(comes)(tell.wait_recv)
    for k in range(chunks):
        kept[k].wait()
        pl.when(left)(lefts[k].wait_send)
        pl.when(right)(lefts[k].wait_recv)
        pl.when(up)(ups[k].wait_send)
        if k < len(corners):
            pl.when(down & left)(corners[k].wait_send)
            pl.when(down & right)(corners[k].wait_recv)
    for clear, there in clears:
        pl.when(there)(clear.wait)


def frame(scan, own):
    chunks, rim = TILE // F, RIM // F
    sems = [4, chunks, chunks, 8, 8, chunks, chunks, rim, rim, 3, 3]
    return pl.pallas_call(
        frame_kernel,
        out_shape=[
            jax.ShapeDtypeStruct((TILE + RIM, TILE + RIM), jnp.bfloat16),
            jax.ShapeDtypeStruct((4,) + own.shape, jnp.int32),
        ],
        in_specs=[pl.BlockSpec(memory_space=pltpu.HBM), pl.BlockSpec(memory_space=pltpu.VMEM)],
        out_specs=[pl.BlockSpec(memory_space=pltpu.HBM), pl.BlockSpec(memory_space=pltpu.VMEM)],
        scratch_shapes=[
            pltpu.VMEM((TILE, TILE), jnp.float32),
            pltpu.VMEM((TILE, TILE), jnp.bfloat16),
            pltpu.VMEM((16, TILE), jnp.bfloat16),
            pltpu.VMEM((TILE, F), jnp.bfloat16),
        ] + [pltpu.SemaphoreType.DMA((n,)) for n in sems],
        compiler_params=pltpu.CompilerParams(
            collective_id=0, has_side_effects=True, vmem_limit_bytes=60 << 20
        ),
    )(scan, own)


def put_taps(ref, row, value):
    value = value.astype(jnp.bfloat16)
    lane = lanes((C, F))
    none = jnp.zeros((), jnp.bfloat16)
    ref[row, 0:C, :] = jnp.where(lane == 0, none, pltpu.roll(value, 1, 1))
    ref[row, C : 2 * C, :] = value
    ref[row, 2 * C : 3 * C, :] = jnp.where(lane == F - 1, none, pltpu.roll(value, F - 1, 1))


def convolved(taps_ref, weight_ref, finish):
    data = jnp.concatenate([taps_ref[k] for k in range(F)], 1)
    out = jnp.dot(weight_ref[...], data, preferred_element_type=jnp.float32)

    def part(tap, k):
        return out[tap * C : (tap + 1) * C, k * F : (k + 1) * F]

    for k in range(F):
        sums = part(1, k)
        if k > 0:
            sums = sums + part(0, k - 1)
        if k < F - 1:
            sums = sums + part(2, k + 1)
        finish(k, sums)


def arrange(stem_raw, first_raw, second_raw, biases_raw, stem_w, first_w, second_w, back_w, biases):
    taps = [stem_raw[k // 7, k % 7].astype(jnp.float32) for k in range(49)]
    turned = jnp.concatenate(taps, 0).T.astype(jnp.bfloat16)
    tap = lax.broadcasted_iota(jnp.int32, (49, 216), 0)
    tap_row, tap_col = tap // 7, tap % 7
    place_col, place_row = lanes((49, 216)) // 24, lanes((49, 216)) % 24
    for r in range(8):
        for q in range(2):
            hit = (place_row == 2 * r + tap_row) & (place_col == 2 * q + tap_col)
            hit = jnp.where(hit, 1.0, 0.0).astype(jnp.bfloat16)
            at = (r * 2 + q) * C
            stem_w[at : at + C, :] = jnp.dot(
                turned, hit, preferred_element_type=jnp.float32
            ).astype(jnp.bfloat16)
    for raw, laid in ((first_raw, first_w), (second_raw, second_w)):
        for dy in range(3):
            block = raw[dy * 3 : dy * 3 + 3].reshape(3 * C, C).astype(jnp.float32)
            laid[dy * C : (dy + 1) * C, :] = block.T.astype(jnp.bfloat16)
    for dy in range(3):
        blocks = [second_raw[(2 - dy) * 3 + (2 - dx)] for dx in range(3)]
        back_w[dy * C : (dy + 1) * C, :] = jnp.concatenate(blocks, 1)
    eye = lax.broadcasted_iota(jnp.int32, (C, C), 0) == lanes((C, C))
    for k in range(3):
        upright = jnp.sum(jnp.where(eye, biases_raw[k][...], 0.0), 1, keepdims=True)
        biases[k] = jnp.broadcast_to(upright, (C, F))


def net_kernel(
    infos, targets, source, stem_raw, first_raw, second_raw,
    stem_bias_raw, first_bias_raw, second_bias_raw, heads, head_bias,
    map_ref, logit_ref,
    stem_w, first_w, second_w, back_w, biases,
    pixels, spread_ref, picked, feats, hidden, grads, acc, order, arrival,
):
    count = jnp.int32(0)
    for slot in range(SLOTS):
        live = infos[0, slot // 2, slot % 2, 0, 0] >= 0

        @pl.when(live)
        def _():
            order[count] = slot

        count = count + live.astype(jnp.int32)

    def place(number):
        slot = order[number]
        turn, which = slot // 2, slot % 2
        top, left = (infos[0, turn, which, 0, k] % TILE for k in range(2))
        return slot, top, left, targets[turn, which, 0]

    def fetch(number):
        _, top, left, _ = place(number)
        row0 = pl.multiple_of(top // 16 * 16, 16)
        col0 = pl.multiple_of(left // F * F, F)
        here = number % 2
        return pltpu.make_async_copy(
            source.at[pl.ds(row0, 528), pl.ds(col0, 640)], pixels.at[here], arrival.at[here]
        )

    @pl.when(count > 0)
    def _():
        fetch(0).start()

    biases_raw = (stem_bias_raw, first_bias_raw, second_bias_raw)
    arrange(
        stem_raw, first_raw, second_raw, biases_raw, stem_w, first_w, second_w, back_w, biases
    )
    map_ref[...] = jnp.zeros_like(map_ref)
    for slot in range(SLOTS):
        logit_ref[slot] = jnp.float32(0.0)

    def window(number, _):
        slot, top, left, target = place(number)

        @pl.when(number + 1 < count)
        def _():
            fetch(number + 1).start()

        over = left % F
        lane = lanes((640, F))
        apart = lax.broadcasted_iota(jnp.int32, (640, F), 0) - over - lane * 4
        for u in range(9):
            hit = apart == u - 3
            if u < 3:
                hit = hit & (lane > 0)
            if u > 6:
                hit = hit & (lane < F - 1)
            spread_ref[:, u * F : (u + 1) * F] = jnp.where(hit, 1.0, 0.0).astype(jnp.bfloat16)
        below = top % 16
        row = lax.broadcasted_iota(jnp.int32, (520, 528), 0) - 3
        shift = jnp.where(
            (lanes((520, 528)) - below == row) & (row >= 0) & (row < WIN), 1.0, 0.0
        ).astype(jnp.bfloat16)
        fetch(number).wait()
        moved = jnp.dot(shift, pixels[number % 2], preferred_element_type=jnp.float32)
        picked[...] = jnp.dot(
            moved.astype(jnp.bfloat16), spread_ref[...], preferred_element_type=jnp.float32
        )
        stem_bias = biases[0]
        lane0 = lanes((C, F)) == 0
        none = jnp.zeros((), jnp.bfloat16)

        def stem():
            even = odd = jnp.full((C, F), LOW, jnp.float32)
            slabs = []
            for k in range(F // 4):
                slab = [
                    picked[k * 16 : k * 16 + 24, u * F : (u + 1) * F] for u in range(9)
                ]
                slabs.append(jnp.concatenate(slab, 0))
            data = jnp.concatenate(slabs, 1).astype(jnp.bfloat16)
            out = jnp.dot(stem_w[...], data, preferred_element_type=jnp.float32)
            for k in range(F // 4):
                for r in range(4):
                    part = lambda n: out[
                        (r * 4 + n) * C : (r * 4 + n + 1) * C, k * F : (k + 1) * F
                    ]
                    e_high = jnp.maximum(jnp.maximum(even, part(0)), part(2))
                    o_high = jnp.maximum(jnp.maximum(odd, part(1)), part(3))
                    even, odd = part(2), part(3)
                    high = jnp.maximum(e_high, o_high) + stem_bias
                    high = jnp.maximum(high, 0.0).astype(jnp.bfloat16)
                    side = jnp.maximum(o_high + stem_bias, 0.0).astype(jnp.bfloat16)
                    before = jnp.where(lane0, none, pltpu.roll(side, 1, 1))
                    put_taps(feats, k * 4 + r, jnp.maximum(high, before))

        stem()

        def after_first(row, sums):
            put_taps(hidden, row, jnp.maximum(sums + biases[1], 0.0))

        convolved(feats, first_w, after_first)

        eye = lax.broadcasted_iota(jnp.int32, (C, C), 0) == lanes((C, C))
        wanted = lax.broadcasted_iota(jnp.int32, (9, C), 0) == target
        head = jnp.where(wanted, heads[...].astype(jnp.float32), 0.0)
        head = jnp.sum(head, 0, keepdims=True)
        column = jnp.sum(jnp.where(eye, head, 0.0), 1, keepdims=True)
        grad = jnp.broadcast_to(
            (column / float(F * F)).astype(jnp.bfloat16).astype(jnp.float32), (C, F)
        )
        acc[...] = jnp.zeros_like(acc)
        held = []

        def after_second(row, sums):
            value = sums + feats[row, C : 2 * C, :].astype(jnp.float32) + biases[2]
            value = jnp.maximum(value, 0.0)
            out = jnp.where(value > 0, grad, 0.0)
            put_taps(grads, row, out)
            held.append((value, out))
            if len(held) == 8:
                acc[0] += sum(kept for kept, _ in held)
                acc[1] += sum(kept for _, kept in held)
                held.clear()

        convolved(hidden, second_w, after_second)

        def after_back(row, sums):
            open_ = hidden[row, C : 2 * C, :].astype(jnp.float32) > 0
            value = jnp.where(open_, sums, 0.0).astype(jnp.bfloat16).astype(jnp.float32)
            if row == 0:
                acc[3] = value
            if row == F - 1:
                acc[4] = value
            held.append(value)
            if len(held) == 8:
                acc[2] += sum(held)
                held.clear()

        convolved(grads, back_w, after_back)

        mean = jnp.sum(acc[0], 1, keepdims=True) / float(F * F)
        logit = jnp.sum(mean * column)
        bias = jnp.sum(jnp.where(lanes((1, 9)) == target, head_bias[...], 0.0))
        logit_ref[slot] = logit + bias

        whole = acc[2]
        parts = [whole - acc[4], whole, whole - acc[3]]
        lane = lanes((C, F))
        channel = jnp.sum(acc[1], 1, keepdims=True)
        for dy in range(3):
            for dx in range(3):
                drop = {0: F - 1, 1: F, 2: 0}[dx]
                total = jnp.sum(jnp.where(lane == drop, 0.0, parts[dy]), 1, keepdims=True)
                flat = jnp.sum(jnp.where(eye, total, 0.0), 0, keepdims=True)
                weight = first_raw[(2 - dy) * 3 + (2 - dx)].astype(jnp.float32)
                channel = channel + jnp.sum(weight * flat, 1, keepdims=True)
        channel = jnp.broadcast_to(channel, (C, F))

        def rows(step, _):
            base = pl.multiple_of(step * 16, 16)
            found = [
                jnp.sum(
                    feats[base + k, C : 2 * C, :].astype(jnp.float32) * channel, 0, keepdims=True
                )
                for k in range(16)
            ]
            found = jnp.maximum(jnp.concatenate(found, 0), 0.0)
            map_ref[slot, pl.ds(base, 16), :] = found.astype(jnp.bfloat16)
            return 0

        lax.fori_loop(0, F // 16, rows, 0)
        return 0

    lax.fori_loop(0, count, window, 0)


def networks(infos, targets, framed, stem_weight, stem_bias, conv1_weight, conv1_bias, conv2_weight,
             conv2_bias, head_weight, head_bias):
    biases = [bias.reshape(1, C) for bias in (stem_bias, conv1_bias, conv2_bias)]
    whole = pl.BlockSpec(memory_space=pltpu.VMEM)
    maps, logits = pl.pallas_call(
        net_kernel,
        in_specs=[pl.BlockSpec(memory_space=pltpu.SMEM)] * 2
        + [pl.BlockSpec(memory_space=pltpu.HBM)] + [whole] * 8,
        out_specs=[whole, pl.BlockSpec(memory_space=pltpu.SMEM)],
        scratch_shapes=[
            pltpu.VMEM((16 * C, 216), jnp.bfloat16),
            pltpu.VMEM((3 * C, 3 * C), jnp.bfloat16),
            pltpu.VMEM((3 * C, 3 * C), jnp.bfloat16),
            pltpu.VMEM((3 * C, 3 * C), jnp.bfloat16),
            pltpu.VMEM((3, C, F), jnp.float32),
            pltpu.VMEM((2, 528, 640), jnp.bfloat16),
            pltpu.VMEM((640, 9 * F), jnp.bfloat16),
            pltpu.VMEM((520, 9 * F), jnp.float32),
            pltpu.VMEM((F, 3 * C, F), jnp.bfloat16),
            pltpu.VMEM((F, 3 * C, F), jnp.bfloat16),
            pltpu.VMEM((F, 3 * C, F), jnp.bfloat16),
            pltpu.VMEM((5, C, F), jnp.float32),
            pltpu.SMEM((SLOTS,), jnp.int32),
            pltpu.SemaphoreType.DMA((2,)),
        ],
        out_shape=[
            jax.ShapeDtypeStruct((SLOTS, F, F), jnp.bfloat16),
            jax.ShapeDtypeStruct((SLOTS,), jnp.float32),
        ],
        compiler_params=pltpu.CompilerParams(vmem_limit_bytes=58 << 20),
    )(
        infos, targets, framed, stem_weight, conv1_weight.reshape(9, C, C),
        conv2_weight.reshape(9, C, C), *biases, head_weight.T, head_bias.reshape(1, 9),
    )
    return maps, logits


def blend_kernel(infos, maps, result, out_ref, total, sems):
    out_ref[...] = jnp.zeros_like(out_ref)
    total[...] = jnp.zeros_like(total)

    def profile(offset):
        value = (offset - (WIN - 1) / 2.0) * (1.0 / (WIN / 4.0))
        return jnp.exp(-0.5 * value * value)

    def window(number, _):
        way, slot = number // SLOTS, number % SLOTS
        turn, which = slot // 2, slot % 2
        corner = infos[way, turn, which, 0, 0]
        top = corner % TILE - way // 2 * TILE
        left = infos[way, turn, which, 0, 1] % TILE - way % 2 * TILE

        @pl.when((corner >= 0) & (top > -WIN) & (left > -WIN))
        def _():
            row0 = pl.multiple_of(jnp.clip(top // 8 * 8, 0, TILE - 520), 8)
            col0 = pl.multiple_of(jnp.clip(left // F * F, 0, TILE - 640), F)
            row = lax.broadcasted_iota(jnp.int32, (520, F), 0) + (row0 - top)
            in_row = (row >= 0) & (row < WIN)
            up = jnp.where(in_row & (row // 4 == lanes((520, F))), 1.0, 0.0)
            down = jnp.where(in_row, profile(row.astype(jnp.float32)), 0.0)
            col = lanes((F, 640)) + (col0 - left)
            in_col = (col >= 0) & (col < WIN)
            tap = lax.broadcasted_iota(jnp.int32, (F, 640), 0)
            across = jnp.where(in_col & (col // 4 == tap), 1.0, 0.0).astype(jnp.bfloat16)
            col = lanes((8, 640)) + (col0 - left)
            in_col = (col >= 0) & (col < WIN)
            side = jnp.where(in_col, profile(col.astype(jnp.float32)), 0.0)[0:1]
            tall = jnp.dot(
                up.astype(jnp.bfloat16), maps[way, slot], preferred_element_type=jnp.float32
            ).astype(jnp.bfloat16)
            for k in range(5):
                part = slice(k * F, (k + 1) * F)
                at = (pl.ds(row0, 520), pl.ds(pl.multiple_of(col0 + k * F, F), F))
                weight = down * side[:, part]
                value = jnp.dot(tall, across[:, part], preferred_element_type=jnp.float32)
                out_ref[at] += value * weight
                total[at] += weight
        return 0

    lax.fori_loop(0, 4 * SLOTS, window, 0)
    copies = []
    for k in range(TILE // F):
        part = slice(k * F, (k + 1) * F)
        out_ref[part, :] = out_ref[part, :] / jnp.maximum(total[part, :], 1.0)
        rows = pl.ds(k * F, F)
        copies.append(pltpu.make_async_copy(out_ref.at[rows], result.at[rows], sems.at[k]))
        copies[-1].start()
    for copy in copies:
        copy.wait()


def blend(infos, maps):
    return pl.pallas_call(
        blend_kernel,
        in_specs=[
            pl.BlockSpec(memory_space=pltpu.SMEM),
            pl.BlockSpec(memory_space=pltpu.VMEM),
        ],
        out_specs=pl.BlockSpec(memory_space=pltpu.HBM),
        scratch_shapes=[
            pltpu.VMEM((TILE, TILE), jnp.float32),
            pltpu.VMEM((TILE, TILE), jnp.float32),
            pltpu.SemaphoreType.DMA((TILE // F,)),
        ],
        out_shape=jax.ShapeDtypeStruct((TILE, TILE), jnp.float32),
        compiler_params=pltpu.CompilerParams(vmem_limit_bytes=40 << 20),
    )(infos, maps)


def share_kernel(maps, every, keep, send, recv):
    row, col = lax.axis_index("row"), lax.axis_index("col")
    rows, cols = lax.axis_size("row"), lax.axis_size("col")
    up, down, left, right = row > 0, row < rows - 1, col > 0, col < cols - 1
    own = pltpu.make_async_copy(maps, every.at[0], keep)
    own.start()
    goes = (right, down, down & right)
    comes = (left, up, up & left)
    barrier = pltpu.get_barrier_semaphore()
    for (by_row, by_col), out, back in zip(WAYS[1:], goes, comes):
        for sign, there in ((1, out), (-1, back)):
            @pl.when(there)
            def _():
                pl.semaphore_signal(
                    barrier, inc=1, device_id=(row + sign * by_row, col + sign * by_col),
                    device_id_type=MESH,
                )
    pl.semaphore_wait(barrier, sum(there.astype(jnp.int32) for there in goes + comes))
    copies = [
        pltpu.make_async_remote_copy(
            src_ref=maps, dst_ref=every.at[k], send_sem=send.at[k - 1], recv_sem=recv.at[k - 1],
            device_id=(row + WAYS[k][0], col + WAYS[k][1]), device_id_type=MESH,
        )
        for k in (1, 2, 3)
    ]
    for k in (2, 1, 0):
        pl.when(goes[k])(copies[k].start)
    own.wait()
    for k in range(3):
        pl.when(goes[k])(copies[k].wait_send)
        pl.when(comes[k])(copies[k].wait_recv)


def share(maps):
    return pl.pallas_call(
        share_kernel,
        out_shape=jax.ShapeDtypeStruct((4,) + maps.shape, maps.dtype),
        in_specs=[pl.BlockSpec(memory_space=pltpu.VMEM)],
        out_specs=pl.BlockSpec(memory_space=pltpu.VMEM),
        scratch_shapes=[
            pltpu.SemaphoreType.DMA,
            pltpu.SemaphoreType.DMA((3,)),
            pltpu.SemaphoreType.DMA((3,)),
        ],
        compiler_params=pltpu.CompilerParams(
            collective_id=1, has_side_effects=True, vmem_limit_bytes=40 << 20
        ),
    )(maps)


def local(scan, anchors, targets, *network):
    own = jnp.pad(anchors, ((0, 0), (0, 0), (0, 0), (0, F - 2)), constant_values=-1)
    framed, infos = frame(scan, own)
    maps, scores = networks(infos, targets, framed, *network)
    saliency = blend(infos, share(maps))
    return saliency, scores.reshape(targets.shape)


def solution(mesh):
    placed = (
        P("row", "col"),
        P(None, "row", "col", None),
        P(None, "row", "col"),
    ) + (P(),) * 8
    return jax.shard_map(
        local,
        mesh=mesh,
        in_specs=placed,
        out_specs=(P("row", "col"), P(None, "row", "col")),
        check_vma=False,
    )
```

profile of v0, /device:TPU:36, one launch (start us, length us, event | category | flops | bytes accessed | tf_op | source)
XLA Modules:
  0.0 106.2 jit_solution(198740869216503670)
XLA Ops:
  0.6 1.3 %pad.4.own = s32[2,2,1,128]{3,2,1,0:T(1,128)} pad(s32[2,2,1,2]{3,2,1,0:T(1,128)} %param.12, s32[]{:T(128)} %constant.0.clone.1), padding=0_0x0_0x0_0x0_126 | pad | bytes 2084 | tf_op jit(solution)/shard_map/jit(_pad)/pad | solution.py:554
  1.9 1.3 %copy.13.targets = s32[2,2,1]{2,1,0:T(2,128)} copy(s32[2,2,1]{1,2,0:T(1,128)} %param.13) | data formatting | bytes 32 | tf_op args[2]
  3.2 1.3 %copy.14.stem_raw = bf16[7,7,1,64]{3,2,1,0:T(2,128)(2,1)} copy(bf16[7,7,1,64]{3,1,2,0:T(8,128)(2,1)} %param.14) | data formatting | bytes 12544 | tf_op args[3]
  4.6 30.1 %shard_map.122 = (bf16[1536,1536]{1,0:T(8,128)(2,1)}, s32[4,2,2,1,128]{4,3,2,1,0:T(1,128)}) custom-call(f32[1024,1024]{1,0:T(8,128)} %scan.1, s32[2,2,1,128]{3,2,1,0:T(1,128)} %pad.4.own), custom_call_target="tpu_custom_call" | custom-call | tf_op jit(solution)/shard_map/pallas_call | solution.py:142
  34.7 0.0 copy-start.1
  34.7 15.5 %shard_map.123 = (bf16[4,128,128]{2,1,0:T(8,128)(2,1)}, f32[4]{0:T(128)}) custom-call(s32[4,2,2,1,128]{4,3,2,1,0:T(1,128)} %get-tuple-element.6.infos, s32[2,2,1]{2,1,0:T(2,128)} %copy.13.targets, bf16[1536,1536]{1,0:T(8,128)(2,1)} %get-tuple-element.7.source, bf16[7,7,1,64]{3,2,1,0:T(2,128)(2,1)} %copy.14.stem_raw, bf16[9,64,64]{2,1,0:T(8,128)(2,1)} %bitcast.8, ...), custom_call_target="tpu_custom_call" | custom-call | tf_op jit(solution)/shard_map/pallas_call | solution.py:398
  50.2 1.3 %reshape.31 = f32[2,2,1]{1,0,2:T(2,128)} reshape(f32[4]{0:T(128)} %get-tuple-element.9) | data formatting | bytes 32 | tf_op jit(solution)/shard_map/reshape | solution.py:558
  51.5 0.0 copy-start
  51.5 0.9 copy-done
  52.4 45.5 %shard_map.124.maps = bf16[4,4,128,128]{3,2,1,0:T(8,128)(2,1)S(1)} custom-call(bf16[4,128,128]{2,1,0:T(8,128)(2,1)S(1)} %copy-done), custom_call_target="tpu_custom_call" | custom-call | tf_op jit(solution)/shard_map/pallas_call | solution.py:537
  97.9 0.0 copy-done.1
  97.9 8.4 %shard_map.125 = f32[1024,1024]{1,0:T(8,128)} custom-call(s32[4,2,2,1,128]{4,3,2,1,0:T(1,128)S(1)} %copy-done.1, bf16[4,4,128,128]{3,2,1,0:T(8,128)(2,1)S(1)} %shard_map.124.maps), custom_call_target="tpu_custom_call" | custom-call | tf_op jit(solution)/shard_map/pallas_call | solution.py:486
Async XLA Ops:
  34.7 63.2 %copy-start.1 = (s32[4,2,2,1,128]{4,3,2,1,0:T(1,128)S(1)}, s32[4,2,2,1,128]{4,3,2,1,0:T(1,128)}, u32[]{:S(2)}) copy-start(s32[4,2,2,1,128]{4,3,2,1,0:T(1,128)} %get-tuple-element.6.infos) | copy-start | bytes 24580
  51.5 0.9 copy-start
where the time goes:
time: 107 us; the launch traced here: 106 us
  Pallas kernels  99.4 us (93%)
  local copies, waits for them, and re-layouts  6.15 us (6%)
    pallas_call x1, Pallas kernels, share(): pl.pallas_call(share_kernel, out_shape=jax.ShapeDtypeStruct((4,) + maps.s...  45.5 us
    pallas_call x1, Pallas kernels, frame(): pl.pallas_call(frame_kernel, out_shape=[jax.ShapeDtypeStruct((TILE + RIM,...  30.1 us
    pallas_call x1, Pallas kernels, networks(): pl.pallas_call(net_kernel, in_specs=[pl.BlockSpec(memory_space=pltpu.SMEM...  15.5 us
    pallas_call x1, Pallas kernels, blend(): pl.pallas_call(blend_kernel, in_specs=[pl.BlockSpec(memory_space=pltpu.SM...  8.38 us
    unnamed x6, local copies, waits for them, and re-layouts  3.58 us

commit v1 on v0

--- a/solution.py
+++ b/solution.py
@@ -334,7 +334,7 @@
             out = jnp.where(value > 0, grad, 0.0)
             put_taps(grads, row, out)
             held.append((value, out))
-            if len(held) == 8:
+            if len(held) == 4:
                 acc[0] += sum(kept for kept, _ in held)
                 acc[1] += sum(kept for _, kept in held)
                 held.clear()
@@ -349,7 +349,7 @@
             if row == F - 1:
                 acc[4] = value
             held.append(value)
-            if len(held) == 8:
+            if len(held) == 4:
                 acc[2] += sum(held)
                 held.clear()
 

time: 107 us -> 96.2 us (0.90)
  Pallas kernels: 99.4 us -> 87.6 us
    pallas_call x1, Pallas kernels: 45.5 us -> 19.8 us  [share(): pl.pallas_call(share_kernel, out_shape=jax.ShapeDtypeStruct((4,) + maps.s...]
    pallas_call x1, Pallas kernels: 15.5 us -> 28.2 us  [networks(): pl.pallas_call(net_kernel, in_specs=[pl.BlockSpec(memory_space=pltpu.SMEM...]
    pallas_call x1, Pallas kernels: 8.38 us -> 9.5 us  [blend(): pl.pallas_call(blend_kernel, in_specs=[pl.BlockSpec(memory_space=pltpu.SM...]
where the time goes in v1:
time: 96.2 us; the launch traced here: 94.4 us
  Pallas kernels  87.6 us (91%)
  local copies, waits for them, and re-layouts  6.15 us (6%)
    pallas_call x1, Pallas kernels, frame(): pl.pallas_call(frame_kernel, out_shape=[jax.ShapeDtypeStruct((TILE + RIM,...  30.1 us
    pallas_call x1, Pallas kernels, networks(): pl.pallas_call(net_kernel, in_specs=[pl.BlockSpec(memory_space=pltpu.SMEM...  28.2 us
    pallas_call x1, Pallas kernels, share(): pl.pallas_call(share_kernel, out_shape=jax.ShapeDtypeStruct((4,) + maps.s...  19.8 us
    pallas_call x1, Pallas kernels, blend(): pl.pallas_call(blend_kernel, in_specs=[pl.BlockSpec(memory_space=pltpu.SM...  9.5 us
    unnamed x6, local copies, waits for them, and re-layouts  3.58 us

profile of v1, /device:TPU:36, one launch (start us, length us, event | category | flops | bytes accessed | tf_op | source)
XLA Modules:
  0.0 94.4 jit_solution(5495729553905239655)
XLA Ops:
  0.6 1.3 %pad.4.own = s32[2,2,1,128]{3,2,1,0:T(1,128)} pad(s32[2,2,1,2]{3,2,1,0:T(1,128)} %param.12, s32[]{:T(128)} %constant.0.clone.1), padding=0_0x0_0x0_0x0_126 | pad | bytes 2084 | tf_op jit(solution)/shard_map/jit(_pad)/pad | solution.py:554
  1.9 1.3 %copy.13.targets = s32[2,2,1]{2,1,0:T(2,128)} copy(s32[2,2,1]{1,2,0:T(1,128)} %param.13) | data formatting | bytes 32 | tf_op args[2]
  3.2 1.3 %copy.14.stem_raw = bf16[7,7,1,64]{3,2,1,0:T(2,128)(2,1)} copy(bf16[7,7,1,64]{3,1,2,0:T(8,128)(2,1)} %param.14) | data formatting | bytes 12544 | tf_op args[3]
  4.6 30.1 %shard_map.122 = (bf16[1536,1536]{1,0:T(8,128)(2,1)}, s32[4,2,2,1,128]{4,3,2,1,0:T(1,128)}) custom-call(f32[1024,1024]{1,0:T(8,128)} %scan.1, s32[2,2,1,128]{3,2,1,0:T(1,128)} %pad.4.own), custom_call_target="tpu_custom_call" | custom-call | tf_op jit(solution)/shard_map/pallas_call | solution.py:142
  34.7 0.0 copy-start.1
  34.7 28.2 %shard_map.123 = (bf16[4,128,128]{2,1,0:T(8,128)(2,1)}, f32[4]{0:T(128)}) custom-call(s32[4,2,2,1,128]{4,3,2,1,0:T(1,128)} %get-tuple-element.6.infos, s32[2,2,1]{2,1,0:T(2,128)} %copy.13.targets, bf16[1536,1536]{1,0:T(8,128)(2,1)} %get-tuple-element.7.source, bf16[7,7,1,64]{3,2,1,0:T(2,128)(2,1)} %copy.14.stem_raw, bf16[9,64,64]{2,1,0:T(8,128)(2,1)} %bitcast.8, ...), custom_call_target="tpu_custom_call" | custom-call | tf_op jit(solution)/shard_map/pallas_call | solution.py:398
  62.9 1.3 %reshape.31 = f32[2,2,1]{1,0,2:T(2,128)} reshape(f32[4]{0:T(128)} %get-tuple-element.9) | data formatting | bytes 32 | tf_op jit(solution)/shard_map/reshape | solution.py:558
  64.2 0.0 copy-start
  64.2 0.9 copy-done
  65.1 19.8 %shard_map.124.maps = bf16[4,4,128,128]{3,2,1,0:T(8,128)(2,1)S(1)} custom-call(bf16[4,128,128]{2,1,0:T(8,128)(2,1)S(1)} %copy-done), custom_call_target="tpu_custom_call" | custom-call | tf_op jit(solution)/shard_map/pallas_call | solution.py:537
  84.9 0.0 copy-done.1
  84.9 9.5 %shard_map.125 = f32[1024,1024]{1,0:T(8,128)} custom-call(s32[4,2,2,1,128]{4,3,2,1,0:T(1,128)S(1)} %copy-done.1, bf16[4,4,128,128]{3,2,1,0:T(8,128)(2,1)S(1)} %shard_map.124.maps), custom_call_target="tpu_custom_call" | custom-call | tf_op jit(solution)/shard_map/pallas_call | solution.py:486
Async XLA Ops:
  34.7 50.2 %copy-start.1 = (s32[4,2,2,1,128]{4,3,2,1,0:T(1,128)S(1)}, s32[4,2,2,1,128]{4,3,2,1,0:T(1,128)}, u32[]{:S(2)}) copy-start(s32[4,2,2,1,128]{4,3,2,1,0:T(1,128)} %get-tuple-element.6.infos) | copy-start | bytes 24580
  64.2 0.9 copy-start
